TPU v7x, 32 devices: a whole 2x2x4 slice. The times are simulated.
32 devices in a mesh: ctx: 8 (over y, x, core), seq: 4 (over z).
Axes of the slice: x: 2, y: 2, z: 4, core: 2. Of those that a mesh axis runs over, the one named last changes fastest.
Arguments:
- lin_query: bfloat16 [2048, 4096], P(('seq', 'ctx')), parts along dimension 0, may hold values from -6 to 6
- lin_keys: bfloat16 [2048, 1024], P(('seq', 'ctx')), parts along dimension 0, may hold values from -6 to 6
- lin_values: bfloat16 [2048, 1024], P(('seq', 'ctx')), parts along dimension 0, may hold values from -6 to 6
- state_in: float32 [32, 128, 128], P('seq'), parts along dimension 0, may hold values from -256 to 256
- norm_gain: float32 [4096], replicated, may hold values from 0.1 to 1.9
- soft_query: bfloat16 [2048, 4096], P(('seq', 'ctx')), parts along dimension 0, may hold values from -7 to 7
- soft_keys: bfloat16 [2048, 1024], P(('seq', 'ctx')), parts along dimension 0, may hold values from -7 to 7
- soft_values: bfloat16 [2048, 1024], P(('seq', 'ctx')), parts along dimension 0, may hold values from -6 to 6
Outputs:
- lin_out: bfloat16 [2048, 4096], P(('seq', 'ctx')), parts along dimension 0
- state_out: float32 [32, 128, 128], P('seq'), parts along dimension 0
- soft_out: bfloat16 [2048, 4096], P(('seq', 'ctx')), parts along dimension 0
There are 4 independent parts, one for each index of `seq`. A program takes and returns all parts, laid end to end along the dimension named above; an argument that names none is the same for every part. Nothing has to cross between parts.
All inputs are finite; a program needn't handle non-finite values.
Results may differ from a plain program's by a relative error of at most 0.014.
Values may be sent and summed in bfloat16 or wider, within the bound.
A program may use at most 64 MiB of HBM per device.

v0:
```python
import jax
import jax.numpy as jnp
from jax import lax
from jax.sharding import PartitionSpec as P


def prefix_2(value, axis, join, neutral):
    count, mine = (lax.axis_size(axis), lax.axis_index(axis))
    pieces = lax.all_gather(value, axis)
    so_far = jnp.full_like(value, 0) + jnp.asarray(neutral, value.dtype)

    def step(position, so_far):
        longer = join(so_far, pieces[position])
        return jnp.where(position < mine, longer, so_far)

    return lax.fori_loop(0, count - 1, step, so_far)


def add_states(earlier, later):
    return earlier + later


def linear_blocks(query, keys, values, state):
    total = query.shape[0]
    block = min(512, total)
    steps = total // block
    heads = query.shape[1]
    width = query.shape[2]
    q_blocks = query.reshape(steps, block, heads, width)
    k_blocks = keys.reshape(steps, block, heads, width)
    v_blocks = values.reshape(steps, block, heads, width)
    lower = jnp.tril(jnp.ones((block, block), jnp.float32))

    def advance(memory, pieces):
        q_block, k_block, v_block = pieces
        carried = jnp.einsum(
            "thd,hde->the", q_block.astype(jnp.float32), memory, precision=lax.Precision.HIGHEST
        )
        inner_scores = (
            jnp.einsum("thd,shd->hts", q_block, k_block, preferred_element_type=jnp.float32) * lower
        )
        inner = jnp.einsum(
            "hts,she->the",
            inner_scores,
            v_block.astype(jnp.float32),
            precision=lax.Precision.HIGHEST,
        )
        update = jnp.einsum("thd,the->hde", k_block, v_block, preferred_element_type=jnp.float32)
        return (memory + update, carried + inner)

    final, outputs = lax.scan(advance, state, (q_blocks, k_blocks, v_blocks))
    return (outputs.reshape(total, heads, width), final)


def head_norm(raw, gain):
    square = jnp.mean(raw * raw, axis=-1, keepdims=True)
    return (raw * lax.rsqrt(square + 1e-06) * gain).astype(jnp.bfloat16)


def causal_softmax(pieces):
    query, keys, values = pieces
    total = query.shape[0]
    heads = query.shape[1]
    width = query.shape[2]
    block = min(512, total)
    steps = total // block
    scale = width ** (-0.5)
    q_blocks = query.reshape(steps, block, heads, width)
    key_pos = jnp.arange(total, dtype=jnp.int32)

    def one_block(parts):
        q_block, offset = parts
        scores = (
            jnp.einsum("qmd,kmd->mqk", q_block, keys, preferred_element_type=jnp.float32) * scale
        )
        query_pos = offset + jnp.arange(block, dtype=jnp.int32)
        allowed = key_pos[None, None, :] <= query_pos[None, :, None]
        scores = jnp.where(allowed, scores, -1e30)
        top = jnp.max(scores, axis=-1, keepdims=True)
        expo = jnp.exp(scores - top)
        weights = (expo / jnp.sum(expo, axis=-1, keepdims=True)).astype(jnp.bfloat16)
        return jnp.einsum(
            "mqk,kmd->qmd", weights, values, preferred_element_type=jnp.float32
        ).astype(jnp.bfloat16)

    offsets = jnp.arange(steps, dtype=jnp.int32) * block
    outputs = lax.map(one_block, (q_blocks, offsets))
    return outputs.reshape(total, heads, width)


def shards(
    lin_query, lin_keys, lin_values, state_in, norm_gain, soft_query, soft_keys, soft_values
):
    rows = lin_query.shape[0]
    kv_heads = state_in.shape[0]
    head_dim = state_in.shape[1]
    heads = lin_query.shape[1] // head_dim
    group = heads // kv_heads
    split = (rows, heads, head_dim)
    shared = (rows, kv_heads, head_dim)
    gain = norm_gain.reshape(heads, head_dim)
    query = lin_query.reshape(split)
    keys = lin_keys.reshape(shared)
    values = lin_values.reshape(shared)
    wide_keys = jnp.repeat(keys, group, axis=1)
    wide_values = jnp.repeat(values, group, axis=1)
    local_state = jnp.einsum("thd,the->hde", keys, values, preferred_element_type=jnp.float32)
    prefix = prefix_2(local_state, "ctx", add_states, jnp.zeros_like(local_state))
    before = jnp.repeat(state_in + prefix, group, axis=0)
    raw, ending = linear_blocks(query, wide_keys, wide_values, before)
    lin_out = head_norm(raw, gain).reshape(rows, heads * head_dim)
    state_out = state_in + lax.psum(local_state.astype(jnp.bfloat16), "ctx").astype(jnp.float32)
    soft_input = (soft_query.astype(jnp.float32) + lin_out.astype(jnp.float32)).astype(jnp.bfloat16)
    soft_k = jnp.repeat(soft_keys.reshape(shared), group, axis=1)
    soft_v = jnp.repeat(soft_values.reshape(shared), group, axis=1)
    attended = causal_softmax(
        (
            lax.all_to_all(
                soft_input.reshape(split), "ctx", split_axis=1, concat_axis=0, tiled=True
            ),
            lax.all_to_all(soft_k, "ctx", split_axis=1, concat_axis=0, tiled=True),
            lax.all_to_all(soft_v, "ctx", split_axis=1, concat_axis=0, tiled=True),
        )
    )
    soft_out = lax.all_to_all(attended, "ctx", split_axis=0, concat_axis=1, tiled=True).reshape(
        rows, heads * head_dim
    )
    return (lin_out, state_out, soft_out)


def solution(mesh):
    in_specs = (
        P(("seq", "ctx"), None),
        P(("seq", "ctx"), None),
        P(("seq", "ctx"), None),
        P("seq", None, None),
        P(),
        P(("seq", "ctx"), None),
        P(("seq", "ctx"), None),
        P(("seq", "ctx"), None),
    )
    out_specs = (P(("seq", "ctx"), None), P("seq", None, None), P(("seq", "ctx"), None))
    return jax.shard_map(shards, mesh=mesh, in_specs=in_specs, out_specs=out_specs, check_vma=False)
```

profile of v0, /device:TPU:0, one launch (start us, length us, event | category | flops | bytes accessed | tf_op | source)
XLA Modules:
  0.0 168.5 jit_solution(18187493341674480513)
XLA Ops:
  7.2 0.0 copy-start
  7.2 0.0 copy-start.2
  7.2 0.0 copy-start.3
  7.2 0.0 all-gather.3.cloned.1.call-start
  7.2 2.2 %fusion.21 = (bf16[8,128,128]{2,1,0:T(8,128)(2,1)}, f32[8,128,128]{2,1,0:T(8,128)}) fusion(bf16[64,1024]{1,0:T(8,128)(2,1)} %param.12, bf16[64,1024]{1,0:T(8,128)(2,1)} %param.11), kind=kOutput, calls=%fused_computation.40 | convolution fusion | flops 16908288 | bytes 1048576 | tf_op jit(solution)/shard_map/thd,the->hde/dot_general | solution.py:107
  9.4 0.0 all-gather.3.cloned.1.call-update
  9.5 0.9 copy_bitcast_fusion.3
  10.4 0.9 broadcast_in_dim.67
  11.3 5.2 %all-to-all-start.1 = ((bf16[64,32,128]{2,0,1:T(8,128)(2,1)}), bf16[64,32,128]{2,0,1:T(8,128)(2,1)}, u32[]{:S(2)}, u32[]{:S(2)}) async-start(bf16[64,32,128]{2,0,1:T(8,128)(2,1)} %bitcast.10), calls=%async_computation.1 | async-start | bytes 1048576 | tf_op jit(solution)/shard_map/all_to_all | solution.py:121
  16.5 0.0 all-reduce.2.cloned.1.call-start
  16.5 0.7 all-reduce.2.cloned.1.call-update
  17.2 0.9 copy_bitcast_fusion.5
  18.2 0.0 copy-done.2
  18.2 0.0 copy-done.3
  18.3 0.1 broadcast_in_dim.62
  18.4 0.0 copy-done
  18.4 0.4 convolution_multiply_fusion
  18.8 0.0 copy-start.1
  18.8 33.4 %all-gather.3.cloned.1.call-done = f32[64,128,128]{2,1,0:T(8,128)} async-done(((f32[8,128,128]{2,1,0:T(8,128)}), f32[64,128,128]{2,1,0:T(8,128)}) %all-gather.3.cloned.1.call-update) | async-done | bytes 4194320 | tf_op jit(solution)/shard_map/all_gather | solution.py:9
  52.2 8.7 %while.9 = (s32[]{:T(128)}, f32[8,128,128]{2,1,0:T(8,128)S(1)}, s32[]{:T(128)}, f32[8,8,128,128]{3,2,1,0:T(8,128)}, s32[]{:T(128)}, /*index=5*/s32[]{:T(128)}) while((s32[]{:T(128)}, f32[8,128,128]{2,1,0:T(8,128)S(1)}, s32[]{:T(128)}, f32[8,8,128,128]{3,2,1,0:T(8,128)}, s32[]{:T(128)}, /*index=5*/s32[]{:T(128)}) %tuple.52), condition=%wide.region_1.2_spmd.clone, body=%wide.region_0.1_spmd.clone.sunk | while | flops 393220 | bytes 1572957 | solution.py:16
  52.2 1.2 add_select_fusion.2
  53.4 1.2 add_select_fusion.2
  54.7 1.2 add_select_fusion.2
  55.9 1.2 add_select_fusion.2
  57.2 1.2 add_select_fusion.2
  58.4 1.2 add_select_fusion.2
  59.7 1.2 add_select_fusion.2
  60.9 48.4 %all-reduce.2.cloned.1.call-done = bf16[8,128,128]{2,1,0:T(8,128)(2,1)} async-done(((bf16[8,128,128]{2,1,0:T(8,128)(2,1)}), bf16[8,128,128]{2,1,0:T(8,128)(2,1)}) %all-reduce.2.cloned.1.call-update) | async-done | bytes 262160 | tf_op jit(solution)/shard_map/psum | solution.py:112
  109.4 0.0 copy-done.1
  109.4 1.8 %convert_add_fusion = (f32[8,128,128]{2,1,0:T(8,128)}, f32[8,128,128]{2,1,0:T(8,128)S(1)}) fusion(f32[8,128,128]{2,1,0:T(8,128)S(1)} %copy-done.1, bf16[8,128,128]{2,1,0:T(8,128)(2,1)} %all-reduce.2.cloned.1.call-done, f32[8,128,128]{2,1,0:T(8,128)S(1)} %get-tuple-element.121), kind=kLoop, calls=%fused_computation.26 | loop fusion | flops 393216 | bytes 2359296 | tf_op jit(solution)/shard_map/add | solution.py:112
  111.2 0.2 broadcast_in_dim.61
  111.5 0.0 copy-start.4
  111.5 1.1 convolution_bitcast_fusion
  112.6 0.1 broadcast_in_dim.65
  112.7 1.0 multiply_reduce_fusion
  113.7 0.0 all-to-all-done.1
  113.7 0.9 broadcast_in_dim.69
  114.6 3.5 %all-to-all-start.2 = ((bf16[64,32,128]{2,0,1:T(8,128)(2,1)}), bf16[64,32,128]{2,0,1:T(8,128)(2,1)S(1)}, u32[]{:S(2)}, u32[]{:S(2)}) async-start(bf16[64,32,128]{2,0,1:T(8,128)(2,1)} %bitcast.14), calls=%async_computation.2 | async-start | bytes 1048576 | tf_op jit(solution)/shard_map/all_to_all | solution.py:122
  118.1 0.0 copy-done.4
  118.1 2.2 %fusion.10 = (bf16[8,32,8,128]{3,2,1,0:T(8,128)(2,1)S(1)}, bf16[64,4096]{1,0:T(8,128)(2,1)}) fusion(bf16[64,4096]{1,0:T(8,128)(2,1)} %param.15, f32[64,32,128]{2,0,1:T(8,128)S(1)} %get-tuple-element.152, f32[32,128]{1,0:T(8,128)S(1)} %bitcast.108, f32[64,32]{0,1:T(8,128)S(1)} %add_rsqrt_fusion), kind=kLoop, calls=%fused_computation.21 | loop fusion | flops 1835008 | bytes 2646016
  120.3 0.9 copy.75
  121.3 6.5 %all-to-all-done.2 = bf16[64,32,128]{2,0,1:T(8,128)(2,1)S(1)} async-done(((bf16[64,32,128]{2,0,1:T(8,128)(2,1)}), bf16[64,32,128]{2,0,1:T(8,128)(2,1)S(1)}, u32[]{:S(2)}, u32[]{:S(2)}) %all-to-all-start.2) | async-done | bytes 524320 | tf_op jit(solution)/shard_map/all_to_all | solution.py:122
  127.8 3.5 %all-to-all-start = ((bf16[64,32,128]{2,0,1:T(8,128)(2,1)}), bf16[64,32,128]{2,0,1:T(8,128)(2,1)S(1)}, u32[]{:S(2)}, u32[]{:S(2)}) async-start(bf16[64,32,128]{2,0,1:T(8,128)(2,1)} %bitcast.95), calls=%async_computation | async-start | bytes 1048576 | tf_op jit(solution)/shard_map/all_to_all | solution.py:118
  131.3 0.1 iota_compare_fusion
  131.4 1.1 copy.40
  132.5 8.5 %all-to-all-done = bf16[64,32,128]{2,0,1:T(8,128)(2,1)S(1)} async-done(((bf16[64,32,128]{2,0,1:T(8,128)(2,1)}), bf16[64,32,128]{2,0,1:T(8,128)(2,1)S(1)}, u32[]{:S(2)}, u32[]{:S(2)}) %all-to-all-start) | async-done | bytes 524320 | tf_op jit(solution)/shard_map/all_to_all | solution.py:118
  141.0 3.6 %fusion.22 = (f32[4,512]{1,0:T(4,128)S(1)}, f32[4,512,512]{1,2,0:T(8,128)}) fusion(pred[512,512]{0,1:T(8,128)(4,1)S(1)} %iota_compare_fusion, bf16[512,4,128]{2,0,1:T(8,128)(2,1)S(1)} %bitcast.107, bf16[512,4,128]{2,0,1:T(8,128)(2,1)S(1)} %bitcast.106), kind=kOutput, calls=%fused_computation.41 | convolution fusion | flops 272630272 | bytes 5513216 | tf_op jit(solution)/shard_map/while/body/eval_jaxpr/sub | solution.py:80
  144.6 3.1 %fusion.8 = bf16[512,4,128]{2,0,1:T(8,128)(2,1)S(1)} fusion(bf16[512,4,128]{2,0,1:T(8,128)(2,1)S(1)} %bitcast.105, f32[4,512,512]{1,2,0:T(8,128)} %get-tuple-element.154, f32[4,512]{1,0:T(4,128)S(1)} %get-tuple-element.153), kind=kOutput, calls=%fused_computation.15 | convolution fusion | flops 270794752 | bytes 5251072 | tf_op jit(solution)/shard_map/while/body/eval_jaxpr/mqk,kmd->qmd/dot_general | solution.py:82
  147.7 0.4 copy.44
  148.1 12.2 %all_to_all.66 = bf16[512,4,128]{2,1,0:T(4,128)(2,1)S(1)} all-to-all(bf16[512,4,128]{2,1,0:T(4,128)(2,1)S(1)} %copy.44), channel_id=1, replica_groups=mesh['ctx'=8,'seq'=4] {'ctx'}, dimensions={0} | all-to-all | bytes 1048576 | tf_op jit(solution)/shard_map/all_to_all | solution.py:125
  160.3 0.2 copy.45
  160.5 1.2 reshape.96
  (7 shorter events, 0.1 us)
Async XLA Ops:
  7.2 11.2 %copy-start = (bf16[64,4096]{1,0:T(8,128)(2,1)S(1)}, bf16[64,4096]{1,0:T(8,128)(2,1)}, u32[]{:S(2)}) copy-start(bf16[64,4096]{1,0:T(8,128)(2,1)} %param.10) | copy-start | bytes 1572868
  7.2 11.0 %copy-start.2 = (bf16[64,1024]{1,0:T(8,128)(2,1)S(1)}, bf16[64,1024]{1,0:T(8,128)(2,1)}, u32[]{:S(2)}) copy-start(bf16[64,1024]{1,0:T(8,128)(2,1)} %param.12) | copy-start | bytes 393220
  7.2 11.0 %copy-start.3 = (bf16[64,1024]{1,0:T(8,128)(2,1)S(1)}, bf16[64,1024]{1,0:T(8,128)(2,1)}, u32[]{:S(2)}) copy-start(bf16[64,1024]{1,0:T(8,128)(2,1)} %param.17) | copy-start | bytes 393220
  7.2 45.0 %all-gather.3.cloned.1.call-start = ((), (), s32[]{:S(2)}) async-start(), calls=%async_computation.5 | async-start | bytes 4718592 | tf_op jit(solution)/shard_map/all_gather | solution.py:9
  11.3 102.4 %all-to-all-start.1 = ((bf16[64,32,128]{2,0,1:T(8,128)(2,1)}), bf16[64,32,128]{2,0,1:T(8,128)(2,1)}, u32[]{:S(2)}, u32[]{:S(2)}) async-start(bf16[64,32,128]{2,0,1:T(8,128)(2,1)} %bitcast.10), calls=%async_computation.1 | async-start | bytes 1048576 | tf_op jit(solution)/shard_map/all_to_all | solution.py:121
  16.5 92.9 %all-reduce.2.cloned.1.call-start = ((), (), s32[]{:S(2)}) async-start(), calls=%async_computation.4 | async-start | bytes 524288 | tf_op jit(solution)/shard_map/psum | solution.py:112
  18.8 90.6 %copy-start.1 = (f32[8,128,128]{2,1,0:T(8,128)S(1)}, f32[8,128,128]{2,1,0:T(8,128)}, u32[]{:S(2)}) copy-start(f32[8,128,128]{2,1,0:T(8,128)} %param.13) | copy-start | bytes 1572868
  111.5 6.7 %copy-start.4 = (f32[4096]{0:T(1024)S(1)}, f32[4096]{0:T(1024)}, u32[]{:S(2)}) copy-start(f32[4096]{0:T(1024)} %param.14) | copy-start | bytes 49156
  114.6 13.2 %all-to-all-start.2 = ((bf16[64,32,128]{2,0,1:T(8,128)(2,1)}), bf16[64,32,128]{2,0,1:T(8,128)(2,1)S(1)}, u32[]{:S(2)}, u32[]{:S(2)}) async-start(bf16[64,32,128]{2,0,1:T(8,128)(2,1)} %bitcast.14), calls=%async_computation.2 | async-start | bytes 1048576 | tf_op jit(solution)/shard_map/all_to_all | solution.py:122
  127.8 13.2 %all-to-all-start = ((bf16[64,32,128]{2,0,1:T(8,128)(2,1)}), bf16[64,32,128]{2,0,1:T(8,128)(2,1)S(1)}, u32[]{:S(2)}, u32[]{:S(2)}) async-start(bf16[64,32,128]{2,0,1:T(8,128)(2,1)} %bitcast.95), calls=%async_computation | async-start | bytes 1048576 | tf_op jit(solution)/shard_map/all_to_all | solution.py:118
Sparse Core Ops, SparseCore 0:
  10.5 41.6 all-gather.2
  55.8 53.5 all-reduce.1
where the time goes:
time: 169 us; the launch traced here: 168 us
  waiting for transfers between devices  97.5 us (58%)
  between operations  14.3 us (8%)
  other arithmetic  12.7 us (8%)
  starting transfers between devices  12.2 us (7%)
  blocking collectives  12.2 us (7%)
  matrix products  11.4 us (7%)
  local copies, waits for them, and re-layouts  8.07 us (5%)
    psum x1, waiting for transfers between devices, shards(): lax.psum(local_state.astype(jnp.bfloat16), 'ctx').astype(jnp.float32)  48.4 us
    all_gather x1, waiting for transfers between devices, prefix_2(): pieces = lax.all_gather(value, axis)  33.4 us
    all_to_all x1, blocking collectives, shards(): lax.all_to_all(attended, 'ctx', split_axis=0, concat_axis=1, tiled=True)  12.2 us
    select_n x7, other arithmetic, step(): return jnp.where(position < mine, longer, so_far)  8.58 us
    all_to_all x1, waiting for transfers between devices, shards(): lax.all_to_all(soft_input.reshape(split), 'ctx', split_axis=1, concat_axi...  8.46 us
    all_to_all x1, waiting for transfers between devices, shards(): lax.all_to_all(soft_v, 'ctx', split_axis=1, concat_axis=0, tiled=True)  6.53 us
    all_to_all x1, starting transfers between devices, shards(): lax.all_to_all(soft_k, 'ctx', split_axis=1, concat_axis=0, tiled=True)  5.17 us
    sub x1, matrix products, one_block(): expo = jnp.exp(scores - top)  3.6 us
  transfers between devices with their start and end apart: 5, of which 4 were waited for; matrix products, arithmetic and copies ran while one was open for 12% of the time, Pallas kernels for 0%

commit v1 on v0

--- a/solution.py
+++ b/solution.py
@@ -1,7 +1,30 @@
+import functools
 import jax
 import jax.numpy as jnp
 from jax import lax
 from jax.sharding import PartitionSpec as P
+
+
+def end_quarters_by_axis(mine_x, array_dim, dim_at):
+    opened, f_next = (lax.axis_size("ctx"), lax.axis_index("ctx"))
+    row_out = mine_x.shape[array_dim] // opened
+    r1 = list(mine_x.shape)
+    r1[array_dim] = row_out
+    n_now = r1[dim_at]
+    r1[dim_at] = n_now * opened
+    big = jnp.zeros(r1, mine_x.dtype)
+    for p in tuple(range(opened)):
+        back = lax.dynamic_slice_in_dim(mine_x, (f_next ^ p) * row_out, row_out, axis=array_dim)
+        if p:
+            crops = []
+            for d in [*range(opened)]:
+                crops.append((d, d ^ p))
+            back = lax.ppermute(back, "ctx", crops)
+        big = lax.dynamic_update_slice_in_dim(big, back, (f_next ^ p) * n_now, axis=dim_at)
+    return big
+
+
+list_the_vector = functools.partial(end_quarters_by_axis, array_dim=1, dim_at=0)
 
 
 def prefix_2(value, axis, join, neutral):
@@ -118,7 +141,7 @@
             lax.all_to_all(
                 soft_input.reshape(split), "ctx", split_axis=1, concat_axis=0, tiled=True
             ),
-            lax.all_to_all(soft_k, "ctx", split_axis=1, concat_axis=0, tiled=True),
+            list_the_vector(soft_k),
             lax.all_to_all(soft_v, "ctx", split_axis=1, concat_axis=0, tiled=True),
         )
     )

time: 169 us -> 164 us (0.970)
  waiting for transfers between devices: 97.5 us -> 85.3 us
  local copies, waits for them, and re-layouts: 8.07 us -> 12.2 us
  starting transfers between devices: 12.2 us -> 15.4 us
    ppermute x0 -> x7, starting transfers between devices: none -> 7.88 us  [end_quarters_by_axis(): back = lax.ppermute(back, 'ctx', crops)]
    all_to_all x1, waiting for transfers between devices: 6.53 us -> 0.01 us  [shards(): lax.all_to_all(soft_v, 'ctx', split_axis=1, concat_axis=0, tiled=True)]
    dynamic_update_slice x0 -> x7, local copies, waits for them, and re-layouts: none -> 6.01 us  [end_quarters_by_axis(): lax.dynamic_update_slice_in_dim(big, back, (f_next ^ p) * n_now, axis=dim...]
    all_to_all x1 -> x0, starting transfers between devices: 5.17 us -> none  [shards(): lax.all_to_all(soft_k, 'ctx', split_axis=1, concat_axis=0, tiled=True)]
    all_to_all x1, waiting for transfers between devices: 8.46 us -> 5.28 us  [shards(): lax.all_to_all(soft_input.reshape(split), 'ctx', split_axis=1, concat_axi...]
    all_gather x1, waiting for transfers between devices: 33.4 us -> 30.9 us  [prefix_2(): pieces = lax.all_gather(value, axis)]
  transfers between devices with their start and end apart: 5 -> 11, of which waited for: 4 -> 3; matrix products, arithmetic and copies ran while one was open for 12% -> 15% of each run, Pallas kernels for 0% -> 0%
where the time goes in v1:
time: 164 us; the launch traced here: 163 us
  waiting for transfers between devices  85.3 us (52%)
  starting transfers between devices  15.4 us (9%)
  between operations  14.5 us (9%)
  local copies, waits for them, and re-layouts  12.2 us (7%)
  blocking collectives  12.2 us (7%)
  other arithmetic  11.8 us (7%)
  matrix products  11.4 us (7%)
    psum x1, waiting for transfers between devices, shards(): lax.psum(local_state.astype(jnp.bfloat16), 'ctx').astype(jnp.float32)  48.4 us
    all_gather x1, waiting for transfers between devices, prefix_2(): pieces = lax.all_gather(value, axis)  30.9 us
    all_to_all x1, blocking collectives, shards(): lax.all_to_all(attended, 'ctx', split_axis=0, concat_axis=1, tiled=True)  12.2 us
    select_n x7, other arithmetic, step(): return jnp.where(position < mine, longer, so_far)  8.58 us
    ppermute x7, starting transfers between devices, end_quarters_by_axis(): back = lax.ppermute(back, 'ctx', crops)  7.88 us
    dynamic_update_slice x7, local copies, waits for them, and re-layouts, end_quarters_by_axis(): lax.dynamic_update_slice_in_dim(big, back, (f_next ^ p) * n_now, axis=dim...  6.01 us
    all_to_all x1, waiting for transfers between devices, shards(): lax.all_to_all(soft_input.reshape(split), 'ctx', split_axis=1, concat_axi...  5.28 us
    all_to_all x1, starting transfers between devices, shards(): lax.all_to_all(soft_v, 'ctx', split_axis=1, concat_axis=0, tiled=True)  3.95 us
  transfers between devices with their start and end apart: 11, of which 3 were waited for; matrix products, arithmetic and copies ran while one was open for 15% of the time, Pallas kernels for 0%

profile of v1, /device:TPU:0, one launch (start us, length us, event | category | flops | bytes accessed | tf_op | source)
XLA Modules:
  0.0 162.9 jit_solution(12418782325654104759)
XLA Ops:
  7.2 0.0 copy-start
  7.2 0.0 all-gather.3.cloned.1.call-start
  7.3 2.2 %fusion.21 = (bf16[8,128,128]{2,1,0:T(8,128)(2,1)}, f32[8,128,128]{2,1,0:T(8,128)}) fusion(bf16[64,1024]{1,0:T(8,128)(2,1)} %param.12, bf16[64,1024]{1,0:T(8,128)(2,1)} %param.11), kind=kOutput, calls=%fused_computation.55 | convolution fusion | flops 16908288 | bytes 1048576 | tf_op jit(solution)/shard_map/thd,the->hde/dot_general | solution.py:130
  9.5 0.0 all-gather.3.cloned.1.call-update
  9.5 0.9 copy_bitcast_fusion.3
  10.5 0.1 broadcast_in_dim.71
  10.6 0.1 broadcast_in_dim.70
  10.7 0.8 constant_dynamic-slice_fusion
  11.4 0.5 collective-permute-start
  11.9 2.5 %collective-permute-start.1 = (bf16[64,4,128]{2,0,1:T(8,128)(2,1)}, bf16[64,4,128]{2,0,1:T(8,128)(2,1)}, u32[]{:S(2)}, u32[]{:S(2)}) collective-permute-start(bf16[64,4,128]{2,0,1:T(8,128)(2,1)} %get-tuple-element.152), channel_id=1, source_target_pairs={{0,8},{4,12},{8,0},{12,4},{16,24},{20,28},{24,16},{28,20},{1,9},{5... | collective-permute-start | bytes 196616 | tf_op jit(solution)/shard_map/ppermute | solution.py:22
  14.4 0.1 collective-permute-start.2
  14.5 1.7 %collective-permute-start.3 = (bf16[64,4,128]{2,0,1:T(8,128)(2,1)}, bf16[64,4,128]{2,0,1:T(8,128)(2,1)}, u32[]{:S(2)}, u32[]{:S(2)}) collective-permute-start(bf16[64,4,128]{2,0,1:T(8,128)(2,1)} %get-tuple-element.150), channel_id=1, source_target_pairs={{0,16},{4,20},{8,24},{12,28},{16,0},{20,4},{24,8},{28,12},{1,17},{... | collective-permute-start | bytes 196616 | tf_op jit(solution)/shard_map/ppermute | solution.py:22
  16.3 0.0 collective-permute-start.4
  16.3 0.9 broadcast_in_dim.73
  17.2 3.9 %all-to-all-start.1 = ((bf16[64,32,128]{2,0,1:T(8,128)(2,1)}), bf16[64,32,128]{2,0,1:T(8,128)(2,1)S(1)}, u32[]{:S(2)}, u32[]{:S(2)}) async-start(bf16[64,32,128]{2,0,1:T(8,128)(2,1)} %bitcast.11), calls=%async_computation.1 | async-start | bytes 1048576 | tf_op jit(solution)/shard_map/all_to_all | solution.py:145
  21.2 0.0 all-reduce.2.cloned.1.call-start
  21.2 0.7 all-reduce.2.cloned.1.call-update
  22.1 0.1 broadcast_in_dim.65
  22.2 0.4 convolution_multiply_fusion
  22.6 0.1 iota_compare_fusion
  22.7 0.0 collective-permute-done
  22.7 3.0 %collective-permute-start.5 = (bf16[64,4,128]{2,0,1:T(8,128)(2,1)}, bf16[64,4,128]{2,0,1:T(8,128)(2,1)}, u32[]{:S(2)}, u32[]{:S(2)}) collective-permute-start(bf16[64,4,128]{2,0,1:T(8,128)(2,1)} %get-tuple-element.148), channel_id=1, source_target_pairs={{0,24},{4,28},{8,16},{12,20},{16,8},{20,12},{24,0},{28,4},{1,25},{... | collective-permute-start | bytes 196616 | tf_op jit(solution)/shard_map/ppermute | solution.py:22
  25.7 0.9 constant_dynamic-update-slice_fusion.5
  26.6 0.0 collective-permute-done.1
  26.6 0.1 collective-permute-start.6
  26.7 0.9 constant_dynamic-update-slice_fusion.4
  27.5 30.9 %all-gather.3.cloned.1.call-done = f32[64,128,128]{2,1,0:T(8,128)} async-done(((f32[8,128,128]{2,1,0:T(8,128)}), f32[64,128,128]{2,1,0:T(8,128)}) %all-gather.3.cloned.1.call-update) | async-done | bytes 4194320 | tf_op jit(solution)/shard_map/all_gather | solution.py:32
  58.4 8.7 %while.9 = (s32[]{:T(128)}, f32[8,128,128]{2,1,0:T(8,128)S(1)}, s32[]{:T(128)}, f32[8,8,128,128]{3,2,1,0:T(8,128)}, s32[]{:T(128)}, /*index=5*/s32[]{:T(128)}) while((s32[]{:T(128)}, f32[8,128,128]{2,1,0:T(8,128)S(1)}, s32[]{:T(128)}, f32[8,8,128,128]{3,2,1,0:T(8,128)}, s32[]{:T(128)}, /*index=5*/s32[]{:T(128)}) %tuple.59), condition=%wide.region_1.2_spmd.clone, body=%wide.region_0.1_spmd.clone.sunk | while | flops 393220 | bytes 1572957 | solution.py:39
  58.4 1.2 add_select_fusion.2
  59.6 1.2 add_select_fusion.2
  60.9 1.2 add_select_fusion.2
  62.1 1.2 add_select_fusion.2
  63.4 1.2 add_select_fusion.2
  64.6 1.2 add_select_fusion.2
  65.9 1.2 add_select_fusion.2
  67.1 48.4 %all-reduce.2.cloned.1.call-done = bf16[8,128,128]{2,1,0:T(8,128)(2,1)} async-done(((bf16[8,128,128]{2,1,0:T(8,128)(2,1)}), bf16[8,128,128]{2,1,0:T(8,128)(2,1)}) %all-reduce.2.cloned.1.call-update) | async-done | bytes 262160 | tf_op jit(solution)/shard_map/psum | solution.py:135
  115.6 2.0 %convert_add_fusion = (f32[8,128,128]{2,1,0:T(8,128)}, f32[8,128,128]{2,1,0:T(8,128)S(1)}) fusion(f32[8,128,128]{2,1,0:T(8,128)} %param.13, bf16[8,128,128]{2,1,0:T(8,128)(2,1)} %all-reduce.2.cloned.1.call-done, f32[8,128,128]{2,1,0:T(8,128)S(1)} %get-tuple-element.121), kind=kLoop, calls=%fused_computation.26 | loop fusion | flops 393216 | bytes 2359296 | tf_op jit(solution)/shard_map/add | solution.py:135
  117.6 0.2 broadcast_in_dim.64
  117.8 0.0 copy-start.1
  117.8 0.0 copy-start.5
  117.8 1.1 convolution_bitcast_fusion
  119.0 0.1 broadcast_in_dim.68
  119.1 0.9 multiply_reduce_fusion
  120.1 1.1 fusion.10
  121.2 0.9 copy.74
  122.2 0.0 all-to-all-done.1
  122.2 3.5 %all-to-all-start = ((bf16[64,32,128]{2,0,1:T(8,128)(2,1)}), bf16[64,32,128]{2,0,1:T(8,128)(2,1)S(1)}, u32[]{:S(2)}, u32[]{:S(2)}) async-start(bf16[64,32,128]{2,0,1:T(8,128)(2,1)} %bitcast.91), calls=%async_computation | async-start | bytes 1048576 | tf_op jit(solution)/shard_map/all_to_all | solution.py:141
  125.7 0.0 collective-permute-done.2
  125.7 0.9 constant_dynamic-update-slice_fusion.3
  126.5 0.0 collective-permute-done.3
  126.5 0.9 constant_dynamic-update-slice_fusion.2
  127.4 0.0 collective-permute-done.4
  127.4 0.9 constant_dynamic-update-slice_fusion.1
  128.3 0.0 collective-permute-done.5
  128.3 0.9 constant_dynamic-update-slice_fusion
  129.1 0.0 collective-permute-done.6
  129.1 0.9 constant_dynamic-update-slice_fusion.6
  130.1 5.3 %all-to-all-done = bf16[64,32,128]{2,0,1:T(8,128)(2,1)S(1)} async-done(((bf16[64,32,128]{2,0,1:T(8,128)(2,1)}), bf16[64,32,128]{2,0,1:T(8,128)(2,1)S(1)}, u32[]{:S(2)}, u32[]{:S(2)}) %all-to-all-start) | async-done | bytes 524320 | tf_op jit(solution)/shard_map/all_to_all | solution.py:141
  135.4 3.6 %fusion.22 = (f32[4,512]{1,0:T(4,128)S(1)}, f32[4,512,512]{1,2,0:T(8,128)}) fusion(pred[512,512]{0,1:T(8,128)(4,1)S(1)} %iota_compare_fusion, bf16[512,4,128]{2,0,1:T(8,128)(2,1)S(1)} %bitcast.103, bf16[512,4,128]{2,0,1:T(8,128)(2,1)S(1)} %constant_dynamic-update-slice_fusion.6), kind=kOutput, calls=%fused_computation.56 | convolution fusion | flops 272630272 | bytes 5513216 | tf_op jit(solution)/shard_map/while/body/eval_jaxpr/sub | solution.py:103
  139.0 3.1 %fusion.8 = bf16[512,4,128]{2,0,1:T(8,128)(2,1)S(1)} fusion(bf16[512,4,128]{2,0,1:T(8,128)(2,1)S(1)} %bitcast.102, f32[4,512,512]{1,2,0:T(8,128)} %get-tuple-element.162, f32[4,512]{1,0:T(4,128)S(1)} %get-tuple-element.161), kind=kOutput, calls=%fused_computation.15 | convolution fusion | flops 270794752 | bytes 5251072 | tf_op jit(solution)/shard_map/while/body/eval_jaxpr/mqk,kmd->qmd/dot_general | solution.py:105
  142.1 0.4 copy.43
  142.5 12.2 %all_to_all.48 = bf16[512,4,128]{2,1,0:T(4,128)(2,1)S(1)} all-to-all(bf16[512,4,128]{2,1,0:T(4,128)(2,1)S(1)} %copy.43), channel_id=1, replica_groups=mesh['ctx'=8,'seq'=4] {'ctx'}, dimensions={0} | all-to-all | bytes 1048576 | tf_op jit(solution)/shard_map/all_to_all | solution.py:148
  154.7 0.2 copy.44
  154.8 1.2 reshape.96
  (17 shorter events, 0.2 us)
Async XLA Ops:
  7.2 15.1 %copy-start = (bf16[64,4096]{1,0:T(8,128)(2,1)S(1)}, bf16[64,4096]{1,0:T(8,128)(2,1)}, u32[]{:S(2)}) copy-start(bf16[64,4096]{1,0:T(8,128)(2,1)} %param.10) | copy-start | bytes 1572868
  7.2 14.8 %copy-start.2 = (bf16[64,1024]{1,0:T(8,128)(2,1)S(1)}, bf16[64,1024]{1,0:T(8,128)(2,1)}, u32[]{:S(2)}) copy-start(bf16[64,1024]{1,0:T(8,128)(2,1)} %param.11) | copy-start | bytes 393220
  7.2 14.8 %copy-start.3 = (bf16[64,1024]{1,0:T(8,128)(2,1)S(1)}, bf16[64,1024]{1,0:T(8,128)(2,1)}, u32[]{:S(2)}) copy-start(bf16[64,1024]{1,0:T(8,128)(2,1)} %param.12) | copy-start | bytes 393220
  7.2 9.1 %copy-start.4 = (bf16[64,1024]{1,0:T(8,128)(2,1)S(1)}, bf16[64,1024]{1,0:T(8,128)(2,1)}, u32[]{:S(2)}) copy-start(bf16[64,1024]{1,0:T(8,128)(2,1)} %param.17) | copy-start | bytes 393220
  7.2 51.2 %all-gather.3.cloned.1.call-start = ((), (), s32[]{:S(2)}) async-start(), calls=%async_computation.4 | async-start | bytes 4718592 | tf_op jit(solution)/shard_map/all_gather | solution.py:32
  11.4 11.3 %collective-permute-start = (bf16[64,4,128]{2,0,1:T(8,128)(2,1)}, bf16[64,4,128]{2,0,1:T(8,128)(2,1)}, u32[]{:S(2)}, u32[]{:S(2)}) collective-permute-start(bf16[64,4,128]{2,0,1:T(8,128)(2,1)} %get-tuple-element.153), channel_id=1, source_target_pairs={{0,4},{4,0},{8,12},{12,8},{16,20},{20,16},{24,28},{28,24},{1,5},{5... | collective-permute-start | bytes 196616 | tf_op jit(solution)/shard_map/ppermute | solution.py:22
  11.9 14.7 %collective-permute-start.1 = (bf16[64,4,128]{2,0,1:T(8,128)(2,1)}, bf16[64,4,128]{2,0,1:T(8,128)(2,1)}, u32[]{:S(2)}, u32[]{:S(2)}) collective-permute-start(bf16[64,4,128]{2,0,1:T(8,128)(2,1)} %get-tuple-element.152), channel_id=1, source_target_pairs={{0,8},{4,12},{8,0},{12,4},{16,24},{20,28},{24,16},{28,20},{1,9},{5... | collective-permute-start | bytes 196616 | tf_op jit(solution)/shard_map/ppermute | solution.py:22
  14.4 111.3 %collective-permute-start.2 = (bf16[64,4,128]{2,0,1:T(8,128)(2,1)}, bf16[64,4,128]{2,0,1:T(8,128)(2,1)}, u32[]{:S(2)}, u32[]{:S(2)}) collective-permute-start(bf16[64,4,128]{2,0,1:T(8,128)(2,1)} %get-tuple-element.151), channel_id=1, source_target_pairs={{0,12},{4,8},{8,4},{12,0},{16,28},{20,24},{24,20},{28,16},{1,13},{... | collective-permute-start | bytes 196616 | tf_op jit(solution)/shard_map/ppermute | solution.py:22
  14.5 112.0 %collective-permute-start.3 = (bf16[64,4,128]{2,0,1:T(8,128)(2,1)}, bf16[64,4,128]{2,0,1:T(8,128)(2,1)}, u32[]{:S(2)}, u32[]{:S(2)}) collective-permute-start(bf16[64,4,128]{2,0,1:T(8,128)(2,1)} %get-tuple-element.150), channel_id=1, source_target_pairs={{0,16},{4,20},{8,24},{12,28},{16,0},{20,4},{24,8},{28,12},{1,17},{... | collective-permute-start | bytes 196616 | tf_op jit(solution)/shard_map/ppermute | solution.py:22
  16.3 111.1 %collective-permute-start.4 = (bf16[64,4,128]{2,0,1:T(8,128)(2,1)}, bf16[64,4,128]{2,0,1:T(8,128)(2,1)}, u32[]{:S(2)}, u32[]{:S(2)}) collective-permute-start(bf16[64,4,128]{2,0,1:T(8,128)(2,1)} %get-tuple-element.149), channel_id=1, source_target_pairs={{0,20},{4,16},{8,28},{12,24},{16,4},{20,0},{24,12},{28,8},{1,21},{... | collective-permute-start | bytes 196616 | tf_op jit(solution)/shard_map/ppermute | solution.py:22
  17.2 104.9 %all-to-all-start.1 = ((bf16[64,32,128]{2,0,1:T(8,128)(2,1)}), bf16[64,32,128]{2,0,1:T(8,128)(2,1)S(1)}, u32[]{:S(2)}, u32[]{:S(2)}) async-start(bf16[64,32,128]{2,0,1:T(8,128)(2,1)} %bitcast.11), calls=%async_computation.1 | async-start | bytes 1048576 | tf_op jit(solution)/shard_map/all_to_all | solution.py:145
  21.2 94.4 %all-reduce.2.cloned.1.call-start = ((), (), s32[]{:S(2)}) async-start(), calls=%async_computation.3 | async-start | bytes 524288 | tf_op jit(solution)/shard_map/psum | solution.py:135
  22.7 105.5 %collective-permute-start.5 = (bf16[64,4,128]{2,0,1:T(8,128)(2,1)}, bf16[64,4,128]{2,0,1:T(8,128)(2,1)}, u32[]{:S(2)}, u32[]{:S(2)}) collective-permute-start(bf16[64,4,128]{2,0,1:T(8,128)(2,1)} %get-tuple-element.148), channel_id=1, source_target_pairs={{0,24},{4,28},{8,16},{12,20},{16,8},{20,12},{24,0},{28,4},{1,25},{... | collective-permute-start | bytes 196616 | tf_op jit(solution)/shard_map/ppermute | solution.py:22
  26.6 102.6 %collective-permute-start.6 = (bf16[64,4,128]{2,0,1:T(8,128)(2,1)}, bf16[64,4,128]{2,0,1:T(8,128)(2,1)}, u32[]{:S(2)}, u32[]{:S(2)}) collective-permute-start(bf16[64,4,128]{2,0,1:T(8,128)(2,1)} %get-tuple-element.147), channel_id=1, source_target_pairs={{0,28},{4,24},{8,20},{12,16},{16,12},{20,8},{24,4},{28,0},{1,29},{... | collective-permute-start | bytes 196616 | tf_op jit(solution)/shard_map/ppermute | solution.py:22
  117.8 2.2 %copy-start.1 = (bf16[64,4096]{1,0:T(8,128)(2,1)S(1)}, bf16[64,4096]{1,0:T(8,128)(2,1)}, u32[]{:S(2)}) copy-start(bf16[64,4096]{1,0:T(8,128)(2,1)} %param.15) | copy-start | bytes 1572868
  117.8 2.2 %copy-start.5 = (f32[4096]{0:T(1024)S(1)}, f32[4096]{0:T(1024)}, u32[]{:S(2)}) copy-start(f32[4096]{0:T(1024)} %param.14) | copy-start | bytes 49156
  122.2 13.2 %all-to-all-start = ((bf16[64,32,128]{2,0,1:T(8,128)(2,1)}), bf16[64,32,128]{2,0,1:T(8,128)(2,1)S(1)}, u32[]{:S(2)}, u32[]{:S(2)}) async-start(bf16[64,32,128]{2,0,1:T(8,128)(2,1)} %bitcast.91), calls=%async_computation | async-start | bytes 1048576 | tf_op jit(solution)/shard_map/all_to_all | solution.py:141
Sparse Core Ops, SparseCore 0:
  10.5 47.8 all-gather.2
  62.0 53.5 all-reduce.1
